TPU v7x, 32 devices: a whole 2x2x4 slice. The times are simulated.
32 devices in a mesh: kvh: 2 (over x), ctx: 16 (over z, y, core).
Axes of the slice: x: 2, y: 2, z: 4, core: 2. Of those that a mesh axis runs over, the one named last changes fastest.
Arguments:
- queries: bfloat16 [512, 32, 128], P('ctx', 'kvh'), parts along dimension 1, may hold values from -6 to 6
- cache_keys: bfloat16 [16384, 256], P('ctx', 'kvh'), parts along dimension 1, may hold values from -6 to 6
- cache_values: bfloat16 [16384, 256], P('ctx', 'kvh'), parts along dimension 1, may hold values from -6 to 6
- span_offset: int32 [1], replicated, may hold values from 0 to 8191
- positions: int32 [512], replicated, may hold values from 0 to 8191
Outputs:
- attended: bfloat16 [512, 32, 128], P('ctx', 'kvh'), parts along dimension 1
There are 2 independent parts, one for each index of `kvh`. A program takes and returns all parts, laid end to end along the dimension named above; an argument that names none is the same for every part. Nothing has to cross between parts.
All inputs are finite; a program needn't handle non-finite values.
Results may differ from a plain program's by a relative error of at most 0.0029.
Values may be sent and summed in bfloat16 or wider, within the bound.
A program may use at most 64 MiB of HBM per device.

v0:
```python
import jax
import jax.numpy as jnp
from jax import lax
from jax.sharding import PartitionSpec as P

masked_floor = -1e30


def local(queries, cache_keys, cache_values, span_offset, positions):
    gathered = lax.all_gather(queries, "ctx", axis=0, tiled=True)
    token_count, head_count, head_width = gathered.shape
    row_count = token_count * head_count
    shard_keys = cache_keys.shape[0]
    key_start = lax.axis_index("ctx") * shard_keys
    key_position = key_start + lax.iota(jnp.int32, shard_keys)
    row_limit = jnp.repeat(span_offset[0] + positions, head_count)
    row_block = 512
    block_count = row_count // row_block
    query_blocks = gathered.reshape(block_count, row_block, head_width)
    limit_blocks = row_limit.reshape(block_count, row_block)
    score_scale = head_width ** (-0.5)

    def shard_partial(inputs):
        query_block, limit_block = inputs
        scores = (
            lax.dot_general(
                query_block,
                cache_keys,
                (((1,), (1,)), ((), ())),
                preferred_element_type=jnp.float32,
            )
            * score_scale
        )
        visible = key_position[None, :] <= limit_block[:, None]
        shard_max = jnp.max(jnp.where(visible, scores, masked_floor), axis=1)
        weights = jnp.where(visible, jnp.exp(scores - shard_max[:, None]), 0.0).astype(jnp.bfloat16)
        shard_den = jnp.sum(weights.astype(jnp.float32), axis=1)
        shard_num = jnp.dot(weights, cache_values, preferred_element_type=jnp.float32)
        return (shard_num, shard_max, shard_den)

    numerator, local_max, denominator = lax.map(shard_partial, (query_blocks, limit_blocks))
    numerator = numerator.reshape(token_count, head_count * head_width)
    local_max = local_max.reshape(token_count, head_count)
    denominator = denominator.reshape(token_count, head_count)
    got_num, got_max, got_den = (
        lax.all_to_all(numerator[None], "ctx", split_axis=1, concat_axis=0, tiled=True),
        lax.all_to_all(local_max[None], "ctx", split_axis=1, concat_axis=0, tiled=True),
        lax.all_to_all(denominator[None], "ctx", split_axis=1, concat_axis=0, tiled=True),
    )
    row_top = jnp.max(got_max, axis=0)
    factor = jnp.exp(got_max - row_top[None])
    sources, own_tokens = (got_max.shape[0], got_max.shape[1])
    num_sum = jnp.sum(
        got_num.reshape(sources, own_tokens, head_count, head_width) * factor[:, :, :, None], axis=0
    )
    den_sum = jnp.sum(got_den * factor, axis=0)
    attended = num_sum / den_sum[:, :, None]
    return attended.astype(jnp.bfloat16)


def solution(mesh):
    in_specs = (P("ctx", "kvh", None), P("ctx", "kvh"), P("ctx", "kvh"), P(), P())
    out_specs = P("ctx", "kvh", None)
    return jax.shard_map(local, mesh=mesh, in_specs=in_specs, out_specs=out_specs, check_vma=False)
```

profile of v0, /device:TPU:13, one launch (start us, length us, event | category | flops | bytes accessed | tf_op | source)
XLA Modules:
  0.0 251.0 jit_solution(5904179462942185829)
XLA Ops:
  9.0 41.6 %all-gather.2.cloned.1.call-done = bf16[512,16,128]{2,1,0:T(8,128)(2,1)} async-done(((bf16[32,16,128]{2,1,0:T(8,128)(2,1)}), bf16[512,16,128]{2,1,0:T(8,128)(2,1)}) %all-gather.2.cloned.1.call-update) | async-done | bytes 2097168 | tf_op jit(solution)/shard_map/all_gather | solution.py:10
  50.6 59.1 %while.15 = (s32[]{:T(128)}, f32[16,512,128]{2,1,0:T(8,128)}, f32[16,512]{1,0:T(8,128)S(1)}, f32[16,512]{1,0:T(8,128)S(1)}, s32[16,512]{1,0:T(8,128)S(1)}, /*ind...) while((s32[]{:T(128)}, f32[16,512,128]{2,1,0:T(8,128)}, ...), condition=%wide.region_3.4_spmd.clone, body=%wide.region_0.3_spmd.clone.sunk | while | flops 274202624 | bytes 8292521 | solution.py:41
  50.6 1.6 fusion.22
  54.3 1.6 fusion.22
  58.0 1.6 fusion.22
  61.7 1.6 fusion.22
  65.4 1.6 fusion.22
  67.9 1.2 fusion.23
  69.1 1.6 fusion.22
  71.6 1.2 fusion.23
  72.8 1.6 fusion.22
  76.4 1.6 fusion.22
  80.1 1.6 fusion.22
  82.7 1.2 fusion.23
  83.8 1.6 fusion.22
  87.5 1.6 fusion.22
  91.2 1.6 fusion.22
  93.7 1.2 fusion.23
  94.9 1.6 fusion.22
  97.4 1.2 fusion.23
  98.6 1.6 fusion.22
  102.3 1.6 fusion.22
  106.0 1.6 fusion.22
  110.3 1.2 reduce.1
  112.3 5.7 %all-to-all-start.2 = ((f32[16,1,512]{2,1,0:T(1,128)}), f32[16,1,512]{2,1,0:T(1,128)S(1)}, u32[]{:S(2)}, u32[]{:S(2)}) async-start(f32[16,1,512]{2,1,0:T(1,128)} %reshape.55), calls=%async_computation.2 | async-start | bytes 65536 | tf_op jit(solution)/shard_map/all_to_all | solution.py:48
  118.1 1.2 reduce.3
  119.5 2.7 %all-to-all-done.2 = f32[16,1,512]{2,1,0:T(1,128)S(1)} async-done(((f32[16,1,512]{2,1,0:T(1,128)}), f32[16,1,512]{2,1,0:T(1,128)S(1)}, u32[]{:S(2)}, u32[]{:S(2)}) %all-to-all-start.2) | async-done | bytes 32800 | tf_op jit(solution)/shard_map/all_to_all | solution.py:48
  122.2 9.2 %all_to_all.36 = f32[16,1,512]{2,1,0:T(1,128)S(1)} all-to-all(f32[16,1,512]{2,1,0:T(1,128)S(1)} %reshape.53), channel_id=1, replica_groups=mesh['kvh'=2,'ctx'=16] {'ctx'}, dimensions={0} | all-to-all | bytes 65536 | tf_op jit(solution)/shard_map/all_to_all | solution.py:47
  131.3 6.9 %all-to-all-start = ((f32[1,512,2048]{2,0,1:T(1,128)}), f32[1,512,2048]{2,0,1:T(1,128)}, u32[]{:S(2)}, u32[]{:S(2)}) async-start(f32[1,512,2048]{2,0,1:T(1,128)} %bitcast.51), calls=%async_computation | async-start | bytes 8388608 | tf_op jit(solution)/shard_map/all_to_all | solution.py:46
  140.6 90.1 %all-to-all-done = f32[1,512,2048]{2,0,1:T(1,128)} async-done(((f32[1,512,2048]{2,0,1:T(1,128)}), f32[1,512,2048]{2,0,1:T(1,128)}, u32[]{:S(2)}, u32[]{:S(2)}) %all-to-all-start) | async-done | bytes 4194336 | tf_op jit(solution)/shard_map/all_to_all | solution.py:46
  230.7 2.5 %mul.33 = f32[16,32,16,128]{3,2,1,0:T(8,128)} broadcast(f32[16,32,16]{2,1,0:T(8,128)S(1)} %get-tuple-element.99), dimensions={0,1,2} | broadcast | bytes 4227072 | tf_op jit(solution)/shard_map/mul | solution.py:54
  233.2 10.0 %multiply_reduce_fusion = f32[32,2048]{1,0:T(8,128)S(1)} fusion(f32[1,16,32,2048]{3,0,2,1:T(1,128)} %bitcast.3, f32[1,16,32,2048]{3,0,2,1:T(1,128)} %bitcast.50), kind=kLoop, calls=%fused_computation.14 | loop fusion | flops 2031616 | bytes 8650752 | tf_op jit(solution)/shard_map/reduce_sum | solution.py:53
  (145 shorter events, 34.3 us)
Async XLA Ops:
  6.5 44.1 %all-gather.2.cloned.1.call-start = ((), (), s32[]{:S(2)}) async-start(), calls=%async_computation.3 | async-start | bytes 2228224 | tf_op jit(solution)/shard_map/all_gather | solution.py:10
  52.2 1.0 copy-start
  55.9 1.0 copy-start
  59.6 1.0 copy-start
  63.2 1.0 copy-start
  66.9 1.0 copy-start
  70.6 1.0 copy-start
  74.3 1.0 copy-start
  78.0 1.0 copy-start
  81.7 1.0 copy-start
  85.4 1.0 copy-start
  89.1 1.0 copy-start
  92.8 1.0 copy-start
  96.5 1.0 copy-start
  100.2 1.0 copy-start
  103.9 1.0 copy-start
  107.6 1.0 copy-start
  112.3 9.9 %all-to-all-start.2 = ((f32[16,1,512]{2,1,0:T(1,128)}), f32[16,1,512]{2,1,0:T(1,128)S(1)}, u32[]{:S(2)}, u32[]{:S(2)}) async-start(f32[16,1,512]{2,1,0:T(1,128)} %reshape.55), calls=%async_computation.2 | async-start | bytes 65536 | tf_op jit(solution)/shard_map/all_to_all | solution.py:48
  131.3 99.4 %all-to-all-start = ((f32[1,512,2048]{2,0,1:T(1,128)}), f32[1,512,2048]{2,0,1:T(1,128)}, u32[]{:S(2)}, u32[]{:S(2)}) async-start(f32[1,512,2048]{2,0,1:T(1,128)} %bitcast.51), calls=%async_computation | async-start | bytes 8388608 | tf_op jit(solution)/shard_map/all_to_all | solution.py:46
Sparse Core Ops, SparseCore 0:
  9.5 41.0 all-gather.1
where the time goes:
time: 252 us; the launch traced here: 251 us
  waiting for transfers between devices  135 us (54%)
  matrix products  43.6 us (17%)
  other arithmetic  26.8 us (11%)
  between operations  14.2 us (6%)
  starting transfers between devices  12.6 us (5%)
  blocking collectives  9.18 us (4%)
  local copies, waits for them, and re-layouts  9.16 us (4%)
    all_to_all x1, waiting for transfers between devices, local(): lax.all_to_all(numerator[None], 'ctx', split_axis=1, concat_axis=0, tiled...  90.1 us
    all_gather x1, waiting for transfers between devices, local(): gathered = lax.all_gather(queries, 'ctx', axis=0, tiled=True)  41.6 us
    dot_general x16, matrix products, shard_partial(): lax.dot_general(query_block, cache_keys, (((1,), (1,)), ((), ())), prefer...  25.1 us
    dot_general x16, matrix products, shard_partial(): jnp.dot(weights, cache_values, preferred_element_type=jnp.float32)  18.4 us
    reduce_sum x16, other arithmetic, shard_partial(): shard_den = jnp.sum(weights.astype(jnp.float32), axis=1)  11.4 us
    reduce_sum x1, other arithmetic, local(): jnp.sum(got_num.reshape(sources, own_tokens, head_count, head_width) * fa...  10 us
    all_to_all x1, blocking collectives, local(): lax.all_to_all(local_max[None], 'ctx', split_axis=1, concat_axis=0, tiled...  9.18 us
    all_to_all x1, starting transfers between devices, local(): lax.all_to_all(numerator[None], 'ctx', split_axis=1, concat_axis=0, tiled...  6.87 us
  transfers between devices with their start and end apart: 3, of which 3 were waited for; matrix products, arithmetic and copies ran while one was open for 2% of the time, Pallas kernels for 0%

commit v1 on v0

v1 whole, which is shorter than its diff:
```python
import functools
import math

import jax
import jax.numpy as jnp
from jax import lax
from jax.experimental import pallas as pl
from jax.experimental.pallas import tpu as pltpu
from jax.sharding import PartitionSpec as P

FLOOR = -1e30
GROUP = 4
LANES = 128


def kernel(n, q_ref, k_ref, v_ref, off_ref, pos_ref, out_ref,
           qbuf, kbuf, vbuf, lim, num, den, top, psend, precv, lsend, lrecv,
           ks_sem, kr_sem, vs_sem, vr_sem, qs_sem, qr_sem, ps_sem, pr_sem, ls_sem, lr_sem):
    rows, width = q_ref.shape
    keys = k_ref.shape[0]
    tokens = pos_ref.shape[0] // (n * GROUP)
    heads = rows // tokens
    tile = min(128, rows)
    tiles = rows // tile
    c = width ** (-0.5) * math.log2(math.e)

    me = lax.axis_index("ctx")
    line = me // GROUP
    spot = me % GROUP
    up, core = spot // 2, spot % 2
    owners = (
        me,
        line * GROUP + up * 2 + (1 - core),
        line * GROUP + (1 - up) * 2 + core,
        line * GROUP + (1 - up) * 2 + (1 - core),
    )

    def ahead(k):
        return lax.rem(line + k, n) * GROUP + spot

    def behind(k):
        return lax.rem(line + n - k, n) * GROUP + spot

    def remote(src, dst, ssem, rsem, to):
        return pltpu.make_async_remote_copy(
            src_ref=src, dst_ref=dst, send_sem=ssem, recv_sem=rsem,
            device_id={"ctx": to}, device_id_type=pl.DeviceIdType.MESH)

    def q_copy(k):
        return remote(q_ref, qbuf.at[k], qs_sem.at[k], qr_sem.at[k], ahead(k))

    def p_copy(k):
        return remote(psend.at[k], precv.at[k], ps_sem.at[k], pr_sem.at[k], behind(k))

    def l_copy(k):
        return remote(lsend.at[k], lrecv.at[k], ls_sem.at[k], lr_sem.at[k], behind(k))

    k_copies = [
        remote(k_ref, kbuf.at[0], ks_sem.at[0], kr_sem.at[0], owners[1]),
        remote(k_ref, kbuf.at[1], ks_sem.at[1], kr_sem.at[1], owners[2]),
        remote(kbuf.at[1], kbuf.at[2], ks_sem.at[2], kr_sem.at[2], owners[1]),
    ]
    v_copies = [
        remote(v_ref, vbuf.at[0], vs_sem.at[0], vr_sem.at[0], owners[1]),
        remote(v_ref, vbuf.at[1], vs_sem.at[1], vr_sem.at[1], owners[2]),
        remote(vbuf.at[1], vbuf.at[2], vs_sem.at[2], vr_sem.at[2], owners[1]),
    ]

    barrier = pltpu.get_barrier_semaphore()
    for to in (owners[1], owners[2]):
        pl.semaphore_signal(barrier, inc=1, device_id={"ctx": to}, device_id_type=pl.DeviceIdType.MESH)

    @pl.loop(1, n)
    def _(k):
        pl.semaphore_signal(barrier, inc=1, device_id={"ctx": ahead(k)}, device_id_type=pl.DeviceIdType.MESH)

    @pl.loop(0, n)
    def _(k):
        first = behind(k) * tokens

        @pl.loop(0, tokens)
        def _(t):
            limit = off_ref[0] + pos_ref[first + t]
            lim[k, pl.ds(pl.multiple_of(t * heads, heads), heads), :] = jnp.full((heads, LANES), limit, jnp.int32)

    qbuf[0] = q_ref[...]
    pl.semaphore_wait(barrier, n + 1)

    k_copies[1].start()
    v_copies[1].start()
    k_copies[0].start()
    v_copies[0].start()

    @pl.loop(1, n)
    def _(k):
        q_copy(k).start()

    lane = lax.broadcasted_iota(jnp.int32, (1, LANES), 1)
    diagonal = (lax.broadcasted_iota(jnp.int32, (tile, LANES), 0)
                == lax.broadcasted_iota(jnp.int32, (tile, LANES), 1))
    ones = jnp.ones((keys, LANES), jnp.bfloat16)

    def block(slot, at, b):
        key_block = k_ref[...] if b == 0 else kbuf[b - 1]
        value_block = v_ref[...] if b == 0 else vbuf[b - 1]
        scores = lax.dot_general(qbuf[slot, at, :], key_block, (((1,), (1,)), ((), ())),
                                 preferred_element_type=jnp.float32)
        limit = lim[slot, at, :]
        base = owners[b] * keys
        parts = []
        for j in range(keys // LANES):
            seen = lane + (base + j * LANES) <= limit
            parts.append(jnp.where(seen, scores[:, j * LANES:(j + 1) * LANES], FLOOR))
        high = functools.reduce(jnp.maximum, parts)
        high = jnp.broadcast_to(jnp.max(high, axis=1, keepdims=True), (tile, LANES))
        weights = jnp.concatenate(
            [jnp.exp2((part - high) * c).astype(jnp.bfloat16) for part in parts], axis=1)
        both = jnp.dot(weights, jnp.concatenate([value_block, ones], axis=1),
                       preferred_element_type=jnp.float32)
        return both[:, :width], both[:, width:], high

    def merge(a, b):
        high = jnp.maximum(a[2], b[2])
        fa, fb = jnp.exp2((a[2] - high) * c), jnp.exp2((b[2] - high) * c)
        return a[0] * fa + b[0] * fb, a[1] * fa + b[1] * fb, high

    def spread(t):
        return pl.ds(pl.multiple_of(t * tile, tile), tile)

    def keep(slot, at, state):
        num[slot, at, :], den[slot, at, :], top[slot, at, :] = state

    def kept(slot, at):
        return num[slot, at, :], den[slot, at, :], top[slot, at, :]

    @pl.loop(0, tiles)
    def _(t):
        keep(0, spread(t), block(0, spread(t), 0))

    k_copies[0].wait_recv()
    v_copies[0].wait_recv()

    @pl.loop(0, tiles)
    def _(t):
        keep(0, spread(t), merge(kept(0, spread(t)), block(0, spread(t), 1)))

    @pl.loop(1, n)
    def _(k):
        q_copy(k).wait_recv()

        @pl.loop(0, tiles)
        def _(t):
            keep(k, spread(t), merge(block(k, spread(t), 0), block(k, spread(t), 1)))

    k_copies[1].wait_recv()
    k_copies[2].start()
    v_copies[1].wait_recv()
    v_copies[2].start()

    @pl.loop(0, n)
    def _(k):
        @pl.loop(0, tiles)
        def _(t):
            keep(k, spread(t), merge(kept(k, spread(t)), block(k, spread(t), 2)))

    k_copies[2].wait_recv()
    v_copies[2].wait_recv()

    @pl.loop(1, n)
    def _(k):
        @pl.loop(0, tiles)
        def _(t):
            at = spread(t)
            top_num, top_den, high = merge(kept(k, at), block(k, at, 3))
            psend[k, at, :] = (top_num / top_den).astype(jnp.bfloat16)
            size = high * c + jnp.log2(top_den)
            lsend[k, pl.ds(t, 1), :] = jnp.sum(jnp.where(diagonal, size, 0.0), axis=0, keepdims=True)

        p_copy(k).start()
        l_copy(k).start()

    @pl.loop(0, tiles)
    def _(t):
        at = spread(t)
        top_num, top_den, high = merge(kept(0, at), block(0, at, 3))
        num[0, at, :] = top_num / top_den
        top[0, at, :] = high * c + jnp.log2(top_den)

    @pl.loop(1, n)
    def _(k):
        p_copy(k).wait_recv()
        l_copy(k).wait_recv()

    @pl.loop(0, tiles)
    def _(t):
        at = spread(t)

        def size_of(k):
            line_of = jnp.broadcast_to(lrecv[k, pl.ds(t, 1), :], (tile, LANES))
            return jnp.broadcast_to(
                jnp.sum(jnp.where(diagonal, line_of, 0.0), axis=1, keepdims=True), (tile, LANES))

        def step(k, state):
            total, mass, high = state
            size = size_of(k)
            higher = jnp.maximum(high, size)
            old, new = jnp.exp2(high - higher), jnp.exp2(size - higher)
            return total * old + precv[k, at, :].astype(jnp.float32) * new, mass * old + new, higher

        state = (num[0, at, :], jnp.ones((tile, LANES), jnp.float32), top[0, at, :])
        if n <= 8:
            for k in range(1, n):
                state = step(k, state)
        else:
            state = lax.fori_loop(1, n, step, state)
        out_ref[at, :] = (state[0] / state[1]).astype(out_ref.dtype)

    for copy in (*k_copies, *v_copies):
        copy.wait_send()

    @pl.loop(1, n)
    def _(k):
        q_copy(k).wait_send()
        p_copy(k).wait_send()
        l_copy(k).wait_send()


def local(n, queries, cache_keys, cache_values, span_offset, positions):
    tokens, heads, width = queries.shape
    rows = tokens * heads
    keys = cache_keys.shape[0]
    tile = min(128, rows)
    marks = max(8, rows // tile)
    vmem = pl.BlockSpec(memory_space=pltpu.VMEM)
    smem = pl.BlockSpec(memory_space=pltpu.SMEM)
    dma = pltpu.SemaphoreType.DMA
    out = pl.pallas_call(
        functools.partial(kernel, n),
        out_shape=jax.ShapeDtypeStruct((rows, width), jnp.bfloat16),
        in_specs=[vmem, vmem, vmem, smem, smem],
        out_specs=vmem,
        scratch_shapes=[
            pltpu.VMEM((n, rows, width), jnp.bfloat16),
            pltpu.VMEM((3, keys, width), jnp.bfloat16),
            pltpu.VMEM((3, keys, width), jnp.bfloat16),
            pltpu.VMEM((n, rows, LANES), jnp.int32),
            pltpu.VMEM((n, rows, width), jnp.float32),
            pltpu.VMEM((n, rows, LANES), jnp.float32),
            pltpu.VMEM((n, rows, LANES), jnp.float32),
            pltpu.VMEM((n, rows, width), jnp.bfloat16),
            pltpu.VMEM((n, rows, width), jnp.bfloat16),
            pltpu.VMEM((n, marks, LANES), jnp.float32),
            pltpu.VMEM((n, marks, LANES), jnp.float32),
            dma((3,)), dma((3,)), dma((3,)), dma((3,)),
            dma((n,)), dma((n,)), dma((n,)), dma((n,)), dma((n,)), dma((n,)),
        ],
        compiler_params=pltpu.CompilerParams(
            collective_id=0, has_side_effects=True, vmem_limit_bytes=40 * 1024 * 1024),
    )(queries.reshape(rows, width), cache_keys, cache_values, span_offset, positions)
    return out.reshape(tokens, heads, width)


def solution(mesh):
    n = mesh.shape["ctx"] // GROUP
    in_specs = (P("ctx", "kvh", None), P("ctx", "kvh"), P("ctx", "kvh"), P(), P())
    return jax.shard_map(functools.partial(local, n), mesh=mesh, in_specs=in_specs,
                         out_specs=P("ctx", "kvh", None), check_vma=False)
```

time: 252 us -> 54.2 us (0.22)
  the two profiles are of different devices: /device:TPU:13 before, /device:TPU:0 now
where the time goes in v1:
time: 54.2 us; the launch traced here: 54 us
  Pallas kernels  49.9 us (92%)
  local copies, waits for them, and re-layouts  3.47 us (6%)
  between operations  0.68 us (1%)
    pallas_call x1, Pallas kernels, local(): pl.pallas_call(functools.partial(kernel, n), out_shape=jax.ShapeDtypeStru...  49.9 us
    unnamed x9, local copies, waits for them, and re-layouts  3.47 us

profile of v1, /device:TPU:0, one launch (start us, length us, event | category | flops | bytes accessed | tf_op | source)
XLA Modules:
  0.0 54.0 jit_solution(14249522718970462482)
XLA Ops:
  0.0 0.0 copy-start.3
  0.7 0.0 copy-done.3
  0.7 0.0 copy-start
  0.7 0.9 %copy-done = bf16[1024,128]{1,0:T(8,128)(2,1)S(1)} copy-done((bf16[1024,128]{1,0:T(8,128)(2,1)S(1)}, bf16[1024,128]{1,0:T(8,128)(2,1)}, u32[]{:S(2)}) %copy-start) | copy-done | bytes 262168
  1.6 0.0 copy-start.1
  1.6 0.9 %copy-done.1 = bf16[1024,128]{1,0:T(8,128)(2,1)S(1)} copy-done((bf16[1024,128]{1,0:T(8,128)(2,1)S(1)}, bf16[1024,128]{1,0:T(8,128)(2,1)}, u32[]{:S(2)}) %copy-start.1) | copy-done | bytes 262168
  2.6 0.0 copy-start.2
  2.6 0.9 %copy-done.2 = bf16[32,16,128]{2,1,0:T(8,128)(2,1)S(1)} copy-done((bf16[32,16,128]{2,1,0:T(8,128)(2,1)S(1)}, bf16[32,16,128]{2,1,0:T(8,128)(2,1)}, u32[]{:S(2)}) %copy-start.2) | copy-done | bytes 131096
  3.5 49.9 %shard_map.55 = bf16[512,128]{1,0:T(8,128)(2,1)S(1)} custom-call(bf16[512,128]{1,0:T(8,128)(2,1)S(1)} %bitcast.3, bf16[1024,128]{1,0:T(8,128)(2,1)S(1)} %copy-done, bf16[1024,128]{1,0:T(8,128)(2,1)S(1)} %copy-done.1, s32[1]{0:T(128)S(6)} %copy.7.off_ref, s32[512]{0:T(512)S(1)} %copy-done.3), custom_call_target="tpu_custom_call" | custom-call | tf_op jit(solution)/shard_map/pallas_call | solution.py:237
  53.4 0.7 %copy.8 = bf16[32,16,128]{2,1,0:T(8,128)(2,1)} copy(bf16[32,16,128]{2,1,0:T(8,128)(2,1)S(1)} %bitcast.2) | data formatting | bytes 262144
Async XLA Ops:
  0.0 0.7 %copy-start.3 = (s32[512]{0:T(512)S(1)}, s32[512]{0:T(512)}, u32[]{:S(2)}) copy-start(s32[512]{0:T(512)} %pos_ref.1) | copy-start | bytes 6148
  0.7 0.9 %copy-start = (bf16[1024,128]{1,0:T(8,128)(2,1)S(1)}, bf16[1024,128]{1,0:T(8,128)(2,1)}, u32[]{:S(2)}) copy-start(bf16[1024,128]{1,0:T(8,128)(2,1)} %k_ref.1) | copy-start | bytes 786436
  1.6 0.9 %copy-start.1 = (bf16[1024,128]{1,0:T(8,128)(2,1)S(1)}, bf16[1024,128]{1,0:T(8,128)(2,1)}, u32[]{:S(2)}) copy-start(bf16[1024,128]{1,0:T(8,128)(2,1)} %v_ref.1) | copy-start | bytes 786436
  2.6 0.9 %copy-start.2 = (bf16[32,16,128]{2,1,0:T(8,128)(2,1)S(1)}, bf16[32,16,128]{2,1,0:T(8,128)(2,1)}, u32[]{:S(2)}) copy-start(bf16[32,16,128]{2,1,0:T(8,128)(2,1)} %param.5) | copy-start | bytes 393220

commit v2 on v1

--- a/solution.py
+++ b/solution.py
@@ -15,13 +15,14 @@
 
 def kernel(n, q_ref, k_ref, v_ref, off_ref, pos_ref, out_ref,
            qbuf, kbuf, vbuf, lim, num, den, top, psend, precv, lsend, lrecv,
-           ks_sem, kr_sem, vs_sem, vr_sem, qs_sem, qr_sem, ps_sem, pr_sem, ls_sem, lr_sem):
+           own_sem, ks_sem, kr_sem, vs_sem, vr_sem, qs_sem, qr_sem, ps_sem, pr_sem, ls_sem, lr_sem):
     rows, width = q_ref.shape
     keys = k_ref.shape[0]
     tokens = pos_ref.shape[0] // (n * GROUP)
     heads = rows // tokens
     tile = min(128, rows)
     tiles = rows // tile
+    unroll = min(4, tiles)
     c = width ** (-0.5) * math.log2(math.e)
 
     me = lax.axis_index("ctx")
@@ -56,15 +57,23 @@
         return remote(lsend.at[k], lrecv.at[k], ls_sem.at[k], lr_sem.at[k], behind(k))
 
     k_copies = [
-        remote(k_ref, kbuf.at[0], ks_sem.at[0], kr_sem.at[0], owners[1]),
-        remote(k_ref, kbuf.at[1], ks_sem.at[1], kr_sem.at[1], owners[2]),
-        remote(kbuf.at[1], kbuf.at[2], ks_sem.at[2], kr_sem.at[2], owners[1]),
+        remote(k_ref, kbuf.at[1], ks_sem.at[0], kr_sem.at[0], owners[1]),
+        remote(k_ref, kbuf.at[2], ks_sem.at[1], kr_sem.at[1], owners[2]),
+        remote(kbuf.at[2], kbuf.at[3], ks_sem.at[2], kr_sem.at[2], owners[1]),
     ]
     v_copies = [
-        remote(v_ref, vbuf.at[0], vs_sem.at[0], vr_sem.at[0], owners[1]),
-        remote(v_ref, vbuf.at[1], vs_sem.at[1], vr_sem.at[1], owners[2]),
-        remote(vbuf.at[1], vbuf.at[2], vs_sem.at[2], vr_sem.at[2], owners[1]),
+        remote(v_ref, vbuf.at[1], vs_sem.at[0], vr_sem.at[0], owners[1]),
+        remote(v_ref, vbuf.at[2], vs_sem.at[1], vr_sem.at[1], owners[2]),
+        remote(vbuf.at[2], vbuf.at[3], vs_sem.at[2], vr_sem.at[2], owners[1]),
     ]
+
+    own_copies = [
+        pltpu.make_async_copy(q_ref, qbuf.at[0], own_sem.at[0]),
+        pltpu.make_async_copy(k_ref, kbuf.at[0], own_sem.at[1]),
+        pltpu.make_async_copy(v_ref, vbuf.at[0], own_sem.at[2]),
+    ]
+    for copy in own_copies:
+        copy.start()
 
     barrier = pltpu.get_barrier_semaphore()
     for to in (owners[1], owners[2]):
@@ -73,6 +82,17 @@
     @pl.loop(1, n)
     def _(k):
         pl.semaphore_signal(barrier, inc=1, device_id={"ctx": ahead(k)}, device_id_type=pl.DeviceIdType.MESH)
+
+    pl.semaphore_wait(barrier, n + 1)
+
+    k_copies[1].start()
+    v_copies[1].start()
+    k_copies[0].start()
+    v_copies[0].start()
+
+    @pl.loop(1, n)
+    def _(k):
+        q_copy(k).start()
 
     @pl.loop(0, n)
     def _(k):
@@ -83,17 +103,8 @@
             limit = off_ref[0] + pos_ref[first + t]
             lim[k, pl.ds(pl.multiple_of(t * heads, heads), heads), :] = jnp.full((heads, LANES), limit, jnp.int32)
 
-    qbuf[0] = q_ref[...]
-    pl.semaphore_wait(barrier, n + 1)
-
-    k_copies[1].start()
-    v_copies[1].start()
-    k_copies[0].start()
-    v_copies[0].start()
-
-    @pl.loop(1, n)
-    def _(k):
-        q_copy(k).start()
+    for copy in own_copies:
+        copy.wait()
 
     lane = lax.broadcasted_iota(jnp.int32, (1, LANES), 1)
     diagonal = (lax.broadcasted_iota(jnp.int32, (tile, LANES), 0)
@@ -101,8 +112,8 @@
     ones = jnp.ones((keys, LANES), jnp.bfloat16)
 
     def block(slot, at, b):
-        key_block = k_ref[...] if b == 0 else kbuf[b - 1]
-        value_block = v_ref[...] if b == 0 else vbuf[b - 1]
+        key_block = kbuf[b]
+        value_block = vbuf[b]
         scores = lax.dot_general(qbuf[slot, at, :], key_block, (((1,), (1,)), ((), ())),
                                  preferred_element_type=jnp.float32)
         limit = lim[slot, at, :]
@@ -133,14 +144,14 @@
     def kept(slot, at):
         return num[slot, at, :], den[slot, at, :], top[slot, at, :]
 
-    @pl.loop(0, tiles)
+    @pl.loop(0, tiles, unroll=unroll)
     def _(t):
         keep(0, spread(t), block(0, spread(t), 0))
 
     k_copies[0].wait_recv()
     v_copies[0].wait_recv()
 
-    @pl.loop(0, tiles)
+    @pl.loop(0, tiles, unroll=unroll)
     def _(t):
         keep(0, spread(t), merge(kept(0, spread(t)), block(0, spread(t), 1)))
 
@@ -148,7 +159,7 @@
     def _(k):
         q_copy(k).wait_recv()
 
-        @pl.loop(0, tiles)
+        @pl.loop(0, tiles, unroll=unroll)
         def _(t):
             keep(k, spread(t), merge(block(k, spread(t), 0), block(k, spread(t), 1)))
 
@@ -157,21 +168,19 @@
     v_copies[1].wait_recv()
     v_copies[2].start()
 
-    @pl.loop(0, n)
-    def _(k):
-        @pl.loop(0, tiles)
-        def _(t):
-            keep(k, spread(t), merge(kept(k, spread(t)), block(k, spread(t), 2)))
+    @pl.loop(0, tiles, unroll=unroll)
+    def _(t):
+        keep(0, spread(t), merge(kept(0, spread(t)), block(0, spread(t), 2)))
 
     k_copies[2].wait_recv()
     v_copies[2].wait_recv()
 
     @pl.loop(1, n)
     def _(k):
-        @pl.loop(0, tiles)
+        @pl.loop(0, tiles, unroll=unroll)
         def _(t):
             at = spread(t)
-            top_num, top_den, high = merge(kept(k, at), block(k, at, 3))
+            top_num, top_den, high = merge(kept(k, at), merge(block(k, at, 2), block(k, at, 3)))
             psend[k, at, :] = (top_num / top_den).astype(jnp.bfloat16)
             size = high * c + jnp.log2(top_den)
             lsend[k, pl.ds(t, 1), :] = jnp.sum(jnp.where(diagonal, size, 0.0), axis=0, keepdims=True)
@@ -179,7 +188,7 @@
         p_copy(k).start()
         l_copy(k).start()
 
-    @pl.loop(0, tiles)
+    @pl.loop(0, tiles, unroll=unroll)
     def _(t):
         at = spread(t)
         top_num, top_den, high = merge(kept(0, at), block(0, at, 3))
@@ -191,7 +200,7 @@
         p_copy(k).wait_recv()
         l_copy(k).wait_recv()
 
-    @pl.loop(0, tiles)
+    @pl.loop(0, tiles, unroll=unroll)
     def _(t):
         at = spread(t)
 
@@ -232,17 +241,18 @@
     tile = min(128, rows)
     marks = max(8, rows // tile)
     vmem = pl.BlockSpec(memory_space=pltpu.VMEM)
+    hbm = pl.BlockSpec(memory_space=pltpu.HBM)
     smem = pl.BlockSpec(memory_space=pltpu.SMEM)
     dma = pltpu.SemaphoreType.DMA
     out = pl.pallas_call(
         functools.partial(kernel, n),
         out_shape=jax.ShapeDtypeStruct((rows, width), jnp.bfloat16),
-        in_specs=[vmem, vmem, vmem, smem, smem],
+        in_specs=[hbm, hbm, hbm, smem, smem],
         out_specs=vmem,
         scratch_shapes=[
             pltpu.VMEM((n, rows, width), jnp.bfloat16),
-            pltpu.VMEM((3, keys, width), jnp.bfloat16),
-            pltpu.VMEM((3, keys, width), jnp.bfloat16),
+            pltpu.VMEM((4, keys, width), jnp.bfloat16),
+            pltpu.VMEM((4, keys, width), jnp.bfloat16),
             pltpu.VMEM((n, rows, LANES), jnp.int32),
             pltpu.VMEM((n, rows, width), jnp.float32),
             pltpu.VMEM((n, rows, LANES), jnp.float32),
@@ -251,11 +261,11 @@
             pltpu.VMEM((n, rows, width), jnp.bfloat16),
             pltpu.VMEM((n, marks, LANES), jnp.float32),
             pltpu.VMEM((n, marks, LANES), jnp.float32),
-            dma((3,)), dma((3,)), dma((3,)), dma((3,)),
+            dma((3,)), dma((3,)), dma((3,)), dma((3,)), dma((3,)),
             dma((n,)), dma((n,)), dma((n,)), dma((n,)), dma((n,)), dma((n,)),
         ],
         compiler_params=pltpu.CompilerParams(
-            collective_id=0, has_side_effects=True, vmem_limit_bytes=40 * 1024 * 1024),
+            collective_id=0, has_side_effects=True, vmem_limit_bytes=56 * 1024 * 1024),
     )(queries.reshape(rows, width), cache_keys, cache_values, span_offset, positions)
     return out.reshape(tokens, heads, width)
 

time: 54.2 us -> 42.8 us (0.79)
  Pallas kernels: 49.9 us -> 40.4 us
  local copies, waits for them, and re-layouts: 3.47 us -> 1.57 us
    pallas_call x1, Pallas kernels: 49.9 us -> 40.4 us  [local(): pl.pallas_call(functools.partial(kernel, n), out_shape=jax.ShapeDtypeStru...]
    unnamed x9 -> x1, local copies, waits for them, and re-layouts: 3.47 us -> 1.57 us
where the time goes in v2:
time: 42.8 us; the launch traced here: 42.6 us
  Pallas kernels  40.4 us (94%)
  local copies, waits for them, and re-layouts  1.57 us (4%)
  between operations  0.66 us (2%)
    pallas_call x1, Pallas kernels, local(): pl.pallas_call(functools.partial(kernel, n), out_shape=jax.ShapeDtypeStru...  40.4 us
    unnamed x1, local copies, waits for them, and re-layouts  1.57 us

profile of v2, /device:TPU:0, one launch (start us, length us, event | category | flops | bytes accessed | tf_op | source)
XLA Modules:
  0.0 42.6 jit_solution(17485109904988631355)
XLA Ops:
  0.7 40.4 %shard_map.55 = bf16[512,128]{1,0:T(8,128)(2,1)} custom-call(bf16[512,128]{1,0:T(8,128)(2,1)} %bitcast.3, bf16[1024,128]{1,0:T(8,128)(2,1)} %k_ref.1, bf16[1024,128]{1,0:T(8,128)(2,1)} %v_ref.1, s32[1]{0:T(128)S(6)} %copy.7.off_ref, s32[512]{0:T(512)} %pos_ref.1), custom_call_target="tpu_custom_call" | custom-call | tf_op jit(solution)/shard_map/pallas_call | solution.py:247
  41.1 1.6 %copy.8 = bf16[32,16,128]{2,1,0:T(8,128)(2,1)} copy(bf16[32,16,128]{2,1,0:T(8,128)(2,1)} %bitcast.2) | data formatting | bytes 262144
